TPU v7x, 32 devices: a whole 2x2x4 slice. The times are simulated.
32 devices in a mesh: seq: 8 (over z, y), dp: 4 (over x, core).
Axes of the slice: x: 2, y: 2, z: 4, core: 2. Of those that a mesh axis runs over, the one named last changes fastest.
Arguments:
- inputs: float32 [4, 4096, 128], P('dp', 'seq'), may hold values from -6 to 6
- gate_values: float32 [4, 4096, 128], P('dp', 'seq'), may hold values from -6 to 6
- out_grad: float32 [4, 4096, 128], P('dp', 'seq'), may hold values from -6 to 6
- filter_taps: float32 [4096, 128], P('seq'), may hold values from -0.09375 to 0.09375
- skip_gain: float32 [128], replicated, may hold values from -4 to 4
Outputs:
- input_grad: float32 [4, 4096, 128], P('dp', 'seq')
- gate_grad: float32 [4, 4096, 128], P('dp', 'seq')
- filter_grad: float32 [4096, 128], P('seq', 'dp')
All inputs are finite; a program needn't handle non-finite values.
Results may differ from a plain program's by a relative error of at most 0.0001.
Values sent between devices are 32-bit elements; how exact they have to be, the bound alone decides.
A program may use at most 64 MiB of HBM per device.

v0:
```python
import functools
import math

import jax
import jax.numpy as jnp
import ml_dtypes
import numpy as np
from jax import lax
from jax.experimental import pallas as pl
from jax.experimental.pallas import tpu as pltpu
from jax.sharding import PartitionSpec as P

first_radix = 32


def rotation(product, modulus, direction):
    fraction = (product % modulus).astype(jnp.float32) / modulus
    turned = 2.0 * math.pi * fraction
    return (jnp.cos(turned), direction * jnp.sin(turned))


def contract(formula, matrix, operand):
    return jnp.einsum(
        formula,
        matrix,
        operand,
        precision=lax.Precision.HIGHEST,
        preferred_element_type=jnp.float32,
    )


def complex_apply(formula, table_re, table_im, values_re, values_im):
    result_re = contract(formula, table_re, values_re) - contract(formula, table_im, values_im)
    result_im = contract(formula, table_re, values_im) + contract(formula, table_im, values_re)
    return (result_re, result_im)


def local_forward(values_re, values_im):
    pairs, rows, width = values_re.shape
    second = rows // first_radix
    values_re = values_re.reshape(pairs, first_radix, second, width)
    values_im = values_im.reshape(pairs, first_radix, second, width)
    outer = jnp.arange(first_radix, dtype=jnp.int32)
    inner = jnp.arange(second, dtype=jnp.int32)
    table_re, table_im = rotation(outer[:, None] * outer[None, :], first_radix, -1.0)
    section_re, section_im = complex_apply(
        "ca,mabx->mcbx", table_re, table_im, values_re, values_im
    )
    twist_re, twist_im = rotation(outer[:, None] * inner[None, :], rows, -1.0)
    twist_re = twist_re[None, :, :, None]
    twist_im = twist_im[None, :, :, None]
    turned_re = section_re * twist_re - section_im * twist_im
    turned_im = section_re * twist_im + section_im * twist_re
    table_re, table_im = rotation(inner[:, None] * inner[None, :], second, -1.0)
    return complex_apply("db,mcbx->mcdx", table_re, table_im, turned_re, turned_im)


def local_inverse(spec_re, spec_im):
    pairs, first, second, width = spec_re.shape
    rows = first * second
    outer = jnp.arange(first, dtype=jnp.int32)
    inner = jnp.arange(second, dtype=jnp.int32)
    table_re, table_im = rotation(inner[:, None] * inner[None, :], second, 1.0)
    section_re, section_im = complex_apply("bd,mcdx->mcbx", table_re, table_im, spec_re, spec_im)
    twist_re, twist_im = rotation(outer[:, None] * inner[None, :], rows, 1.0)
    twist_re = twist_re[None, :, :, None]
    twist_im = twist_im[None, :, :, None]
    turned_re = section_re * twist_re - section_im * twist_im
    turned_im = section_re * twist_im + section_im * twist_re
    table_re, table_im = rotation(outer[:, None] * outer[None, :], first, 1.0)
    result_re, result_im = complex_apply("ac,mcbx->mabx", table_re, table_im, turned_re, turned_im)
    return (result_re.reshape(pairs, rows, width), result_im.reshape(pairs, rows, width))


def frequency_labels():
    steps = lax.axis_size("seq")
    own = lax.axis_index("seq")
    local_labels = 2 * own + jnp.arange(2, dtype=jnp.int32)
    all_labels = jnp.arange(2 * steps, dtype=jnp.int32)
    return (local_labels, all_labels)


def forward_spectrum(signal):
    rows, width = signal.shape
    steps = lax.axis_size("seq")
    piece = rows // steps
    double = 2 * steps
    total = double * rows
    columns = lax.all_to_all(
        signal.reshape(1, rows, width), "seq", split_axis=1, concat_axis=0, tiled=True
    )
    block_index = jnp.arange(steps, dtype=jnp.int32)
    freq_index = jnp.arange(double, dtype=jnp.int32)
    table_re, table_im = rotation(freq_index[:, None] * block_index[None, :], double, -1.0)
    coarse_re = contract("kq,qrc->krc", table_re, columns)
    coarse_im = contract("kq,qrc->krc", table_im, columns)
    offsets = lax.axis_index("seq") * piece + jnp.arange(piece, dtype=jnp.int32)
    twist_re, twist_im = rotation(freq_index[:, None] * offsets[None, :], total, -1.0)
    twist_re = twist_re[:, :, None]
    twist_im = twist_im[:, :, None]
    turned_re = coarse_re * twist_re - coarse_im * twist_im
    turned_im = coarse_re * twist_im + coarse_im * twist_re
    moved = lax.all_to_all(
        jnp.stack([turned_re, turned_im]), "seq", split_axis=1, concat_axis=2, tiled=True
    )
    return local_forward(moved[0], moved[1])


def inverse_time(spec_re, spec_im, local_labels, all_labels):
    pairs, first, second, width = spec_re.shape
    rows = first * second
    steps = lax.axis_size("seq")
    double = 2 * steps
    total = double * rows
    time_re, time_im = local_inverse(spec_re, spec_im)
    positions = jnp.arange(rows, dtype=jnp.int32)
    twist_re, twist_im = rotation(local_labels[:, None] * positions[None, :], total, 1.0)
    twist_re = twist_re[:, :, None]
    twist_im = twist_im[:, :, None]
    turned_re = time_re * twist_re - time_im * twist_im
    turned_im = time_re * twist_im + time_im * twist_re
    moved = lax.all_to_all(
        jnp.stack([turned_re, turned_im]), "seq", split_axis=2, concat_axis=1, tiled=True
    )
    block_index = jnp.arange(steps, dtype=jnp.int32)
    table_re, table_im = rotation(block_index[:, None] * all_labels[None, :], double, 1.0)
    result_re = (
        contract("qk,krc->qrc", table_re, moved[0]) - contract("qk,krc->qrc", table_im, moved[1])
    ) / total
    result_im = (
        contract("qk,krc->qrc", table_re, moved[1]) + contract("qk,krc->qrc", table_im, moved[0])
    ) / total
    return (result_re, result_im)


def local(inputs, gate_values, out_grad, filter_taps, skip_gain):
    seq_input = inputs[0]
    seq_gate = gate_values[0]
    seq_grad = out_grad[0]
    rows, width = seq_input.shape
    replicas = lax.axis_size("dp")
    conv_grad = seq_grad * seq_gate
    spec_re, spec_im = forward_spectrum(
        jnp.concatenate([seq_input, conv_grad, filter_taps], axis=1)
    )
    filter_re = spec_re[..., 2 * width :]
    filter_im = spec_im[..., 2 * width :]
    input_re = spec_re[..., :width]
    input_im = spec_im[..., :width]
    grad_re = spec_re[..., width : 2 * width]
    grad_im = spec_im[..., width : 2 * width]
    conv_re = filter_re * input_re - filter_im * input_im
    conv_im = filter_re * input_im + filter_im * input_re
    corr_re = filter_re * grad_re + filter_im * grad_im
    corr_im = filter_re * grad_im - filter_im * grad_re
    taps_re = input_re * grad_re + input_im * grad_im
    taps_im = input_re * grad_im - input_im * grad_re
    packed_re = conv_re - corr_im
    packed_im = conv_im + corr_re
    local_labels, all_labels = frequency_labels()
    result_re, result_im = inverse_time(
        jnp.concatenate([packed_re, taps_re], axis=3),
        jnp.concatenate([packed_im, taps_im], axis=3),
        local_labels,
        all_labels,
    )
    results = jnp.concatenate([result_re, result_im[..., :width]], axis=2)
    timeline = lax.all_to_all(results, "seq", split_axis=0, concat_axis=1, tiled=True)[0]
    conv_time = timeline[:, :width]
    corr_time = timeline[:, timeline.shape[1] - width :]
    taps_time = timeline[:, width : timeline.shape[1] - width]
    taps_time = lax.psum_scatter(taps_time, "dp", scatter_dimension=1, tiled=True)
    gate_part = seq_grad * (conv_time + skip_gain[None, :] * seq_input)
    input_part = corr_time + skip_gain[None, :] * conv_grad
    length_total = rows * lax.axis_size("seq")
    batch_total = replicas * inputs.shape[0]
    filter_part = taps_time / math.sqrt(batch_total * length_total)
    return (input_part[None], gate_part[None], filter_part)


MESH = pl.DeviceIdType.MESH


def split_halves(table):
    high = table.astype(ml_dtypes.bfloat16)
    low = (table - high.astype(np.float64)).astype(ml_dtypes.bfloat16)
    return high, low


def block_tables(rows):
    double = 2 * rows
    place = np.arange(rows)
    turned = 2.0 * np.pi * ((place[:, None] * place[None, :]) % double) / double
    real = np.cos(turned)
    imag = -np.sin(turned)
    imag[:, 0] = 1.0 - 2.0 * (place % 2)
    forward = np.concatenate([real, imag], axis=1)
    weight = np.full((double, 1), 2.0 / double)
    weight[0] = weight[rows] = 1.0 / double
    inverse = forward.T * weight
    return split_halves(forward) + split_halves(inverse)


def dot3(values, high, low):
    top = values.astype(jnp.bfloat16)
    rest = (values - top.astype(jnp.float32)).astype(jnp.bfloat16)
    dot = functools.partial(jnp.dot, preferred_element_type=jnp.float32)
    return dot(top, high) + (dot(rest, high) + dot(top, low))


def kernel(
    steps, replicas, batch_total,
    in_any, gate_any, og_any, taps_any, skip_any, fh_any, fl_any, ih_any, il_any,
    ig_ref, gg_ref, fg_ref,
    inp, gate, og, taps, skip, fh, fl, ih, il,
    tall, tsend, trecv, xsend, xrecv, gsend, grecv,
    rows8, trows8, spec_t, spec_x, spec_g, prod, tprod,
    csend, crecv, rsend, rrecv, bsend, brecv, merged,
    load_sem, tsend_sem, trecv_sem, xsend_sem, xrecv_sem, gsend_sem, grecv_sem,
    csend_sem, crecv_sem, rsend_sem, rrecv_sem, bsend_sem, brecv_sem,
):
    devices = steps * replicas
    pairs = replicas // 2
    own_s = lax.axis_index("seq")
    own_d = lax.axis_index("dp")
    me = own_s * replicas + own_d
    group = own_d * steps + own_s
    rows, width = inp.shape
    lanes = 128
    half = 4

    barrier = pltpu.get_barrier_semaphore()

    def greet(i, carry):
        p = lax.rem(me + i, devices)
        pl.semaphore_signal(
            barrier, inc=1, device_id=(p // replicas, lax.rem(p, replicas)), device_id_type=MESH
        )
        return carry

    loads = [
        pltpu.make_async_copy(src, dst, load_sem.at[k])
        for k, (src, dst) in enumerate([
            (taps_any, taps), (in_any, inp), (og_any, og), (gate_any, gate), (skip_any, skip),
            (fh_any, fh), (fl_any, fl), (ih_any, ih), (il_any, il),
        ])
    ]
    for copy in loads:
        copy.start()
    lax.fori_loop(1, devices, greet, 0)

    def seq_copy(src, dst, src_sem, dst_sem, s, q):
        return pltpu.make_async_remote_copy(
            src_ref=src.at[s], dst_ref=dst.at[q], send_sem=src_sem.at[s],
            recv_sem=dst_sem.at[q], device_id=(s, own_d), device_id_type=MESH,
        )

    def out_copy(src, dst, src_sem, dst_sem, p, q):
        s, d = p // replicas, lax.rem(p, replicas)
        return pltpu.make_async_remote_copy(
            src_ref=src.at[d * steps + s], dst_ref=dst.at[q // replicas, lax.rem(q, replicas)],
            send_sem=src_sem.at[p], recv_sem=dst_sem.at[q], device_id=(s, d), device_id_type=MESH,
        )

    def back_copy(src, dst, src_sem, dst_sem, p, q):
        s, d = p // replicas, lax.rem(p, replicas)
        return pltpu.make_async_remote_copy(
            src_ref=src.at[s, d], dst_ref=dst.at[lax.rem(q, replicas) * steps + q // replicas],
            send_sem=src_sem.at[p], recv_sem=dst_sem.at[q], device_id=(s, d), device_id_type=MESH,
        )

    def over_seq(use):
        def body(i, carry):
            use(lax.rem(own_s + i, steps))
            return carry

        lax.fori_loop(1, steps, body, 0)

    def over_all(use):
        def body(i, carry):
            use(lax.rem(me + stride * i, devices))
            return carry

        lax.fori_loop(1, devices, body, 0)

    t_refs = (tsend, trecv, tsend_sem, trecv_sem)
    x_refs = (xsend, xrecv, xsend_sem, xrecv_sem)
    g_refs = (gsend, grecv, gsend_sem, grecv_sem)
    c_refs = (csend, crecv, csend_sem, crecv_sem)
    r_refs = (rsend, rrecv, rsend_sem, rrecv_sem)
    b_refs = (bsend, brecv, bsend_sem, brecv_sem)

    def to_channels(values, ref):
        turned = values.T
        for k in range(width // half):
            ref[k] = turned[half * k : half * k + half]

    loads[0].wait()
    tall[...] = taps[...].T.reshape(replicas, steps * half, rows)
    mine = tall[own_d]
    for k in range(steps):
        tsend[k] = mine[half * k : half * k + half]
    loads[1].wait()
    to_channels(inp[...], xsend)
    pl.semaphore_wait(barrier, devices - 1)
    over_seq(lambda s: seq_copy(*t_refs, s, own_s).start())
    over_all(lambda p: out_copy(*x_refs, p, me).start())
    loads[2].wait()
    loads[3].wait()
    gate[...] = og[...] * gate[...]
    to_channels(gate[...], gsend)
    over_all(lambda p: out_copy(*g_refs, p, me).start())
    trecv[own_s] = tsend[own_s]
    xrecv[own_s, own_d] = xsend[group]
    grecv[own_s, own_d] = gsend[group]
    for copy in loads[4:]:
        copy.wait()

    lane = lax.broadcasted_iota(jnp.int32, (8, lanes), 1)
    sign = (1 - 2 * lax.rem(lane, 2)).astype(jnp.float32)

    def forward(ref, spec):
        for s in range(steps):
            for d in range(replicas):
                at = half * (d % 2)
                rows8[s * pairs + d // 2, at : at + half] = ref[s, d]
        spec[...] = dot3(rows8[...].reshape(steps * pairs * 8, rows), fh[...], fl[...]).reshape(
            steps, pairs, 8, 2 * rows
        )

    def backward(ref):
        result = dot3(prod[...].reshape(steps * pairs * 8, 2 * rows), ih[...], il[...])
        for s in range(steps):
            for d in range(replicas):
                at = half * (replicas * s + d)
                ref[s, d] = result[at : at + half]

    def slices(c):
        re_at = pl.ds(pl.multiple_of(c * lanes, lanes), lanes)
        im_at = pl.ds(pl.multiple_of(rows + c * lanes, lanes), lanes)
        return re_at, im_at, (lane + c * lanes) == 0

    def shifted(re, im, first):
        out_re = [re[0]] + [re[j] + sign * re[j - 1] for j in range(1, steps)]
        out_im = [im[0]] + [im[j] + sign * im[j - 1] for j in range(1, steps)]
        out_re2 = [jnp.where(first, b, a) for a, b in zip(out_re, out_im)]
        return out_re, [jnp.where(first, 0.0, b) for b in out_im], out_re2

    def add(total, term):
        return term if total is None else total + term

    def filter_blocks(re_at, im_at, first):
        return shifted(
            [spec_t[j, :, re_at] for j in range(steps)], [spec_t[j, :, im_at] for j in range(steps)], first
        )

    def blocks(spec, k, at):
        return [spec[j, k, :, at] for j in range(steps)]

    def convolve(c, carry):
        re_at, im_at, first = slices(c)
        h_re, h_im, h_re2 = filter_blocks(re_at, im_at, first)
        for k in range(pairs):
            x_re, x_im = blocks(spec_x, k, re_at), blocks(spec_x, k, im_at)
            for u in range(steps):
                re, im = None, None
                for v in range(u + 1):
                    j = u - v
                    re = add(re, h_re[j] * x_re[v] - h_im[j] * x_im[v])
                    im = add(im, h_re2[j] * x_im[v] + h_im[j] * x_re[v])
                prod[u, k, :, re_at] = re
                prod[u, k, :, im_at] = im
        return carry

    def correlate(c, carry):
        re_at, im_at, first = slices(c)
        h_re, h_im, h_re2 = filter_blocks(re_at, im_at, first)
        for k in range(pairs):
            g_re, g_im = blocks(spec_g, k, re_at), blocks(spec_g, k, im_at)
            for u in range(steps):
                re, im = None, None
                for v in range(u, steps):
                    j = v - u
                    re = add(re, h_re[j] * g_re[v] + h_im[j] * g_im[v])
                    im = add(im, h_re2[j] * g_im[v] - h_im[j] * g_re[v])
                prod[u, k, :, re_at] = re
                prod[u, k, :, im_at] = im
        return carry

    def correlate_taps(c, carry):
        re_at, im_at, first = slices(c)
        sums_re, sums_im = [None] * steps, [None] * steps
        for k in range(pairs):
            x_re, x_im, x_re2 = shifted(blocks(spec_x, k, re_at), blocks(spec_x, k, im_at), first)
            g_re, g_im = blocks(spec_g, k, re_at), blocks(spec_g, k, im_at)
            for u in range(steps):
                for v in range(u, steps):
                    j = v - u
                    sums_re[u] = add(sums_re[u], g_re[v] * x_re[j] + g_im[v] * x_im[j])
                    sums_im[u] = add(sums_im[u], g_im[v] * x_re2[j] - g_re[v] * x_im[j])
        for u in range(steps):
            tprod[u, :, re_at] = sums_re[u] + pltpu.roll(sums_re[u], half, 0)
            tprod[u, :, im_at] = sums_im[u] + pltpu.roll(sums_im[u], half, 0)
        return carry

    def to_positions(ref):
        for k in range(width // half):
            at = half * (k % 2)
            merged[k // 2, at : at + half] = ref[k]
        return merged[...].reshape(width, rows).T

    over_seq(lambda s: seq_copy(*t_refs, s, s).wait_recv())
    for k in range(steps):
        trows8[k, :half] = trecv[k]
        trows8[k, half:] = trecv[k]
    spec_t[...] = dot3(trows8[...].reshape(steps * 8, rows), fh[...], fl[...]).reshape(steps, 8, 2 * rows)

    over_all(lambda p: out_copy(*x_refs, p, p).wait_recv())
    forward(xrecv, spec_x)
    lax.fori_loop(0, rows // lanes, convolve, 0)
    backward(csend)
    over_all(lambda p: back_copy(*c_refs, p, me).start())

    over_all(lambda p: out_copy(*g_refs, p, p).wait_recv())
    forward(grecv, spec_g)
    lax.fori_loop(0, rows // lanes, correlate, 0)
    backward(rsend)
    over_all(lambda p: back_copy(*r_refs, p, me).start())

    lax.fori_loop(0, rows // lanes, correlate_taps, 0)
    folded = dot3(tprod[...].reshape(steps * 8, 2 * rows), ih[...], il[...])
    for k in range(steps):
        bsend[k] = folded[8 * k : 8 * k + half]
    over_seq(lambda s: seq_copy(*b_refs, s, own_s).start())

    crecv[group] = csend[own_s, own_d]
    rrecv[group] = rsend[own_s, own_d]
    brecv[own_s] = bsend[own_s]

    over_all(lambda p: back_copy(*c_refs, p, p).wait_recv())
    gain = skip[...]
    gg_ref[...] = og[...] * (to_positions(crecv) + gain * inp[...])
    over_all(lambda p: back_copy(*r_refs, p, p).wait_recv())
    ig_ref[...] = to_positions(rrecv) + gain * gate[...]
    over_seq(lambda s: seq_copy(*b_refs, s, s).wait_recv())
    scale = 1.0 / math.sqrt(batch_total * rows * steps)
    fg_ref[...] = scale * jnp.concatenate([brecv[k] for k in range(steps)], axis=0)

    over_seq(lambda s: seq_copy(*t_refs, s, s).wait_send())
    over_seq(lambda s: seq_copy(*b_refs, s, s).wait_send())
    over_all(lambda p: out_copy(*x_refs, p, p).wait_send())
    over_all(lambda p: out_copy(*g_refs, p, p).wait_send())
    over_all(lambda p: back_copy(*c_refs, p, p).wait_send())
    over_all(lambda p: back_copy(*r_refs, p, p).wait_send())


stride = 1


def fused(inputs, gate_values, out_grad, filter_taps, skip_gain, steps, replicas):
    rows, width = filter_taps.shape
    devices = steps * replicas
    pairs = replicas // 2
    double = 2 * rows
    tables = block_tables(rows)
    f32, bf16 = jnp.float32, jnp.bfloat16
    dma = pltpu.SemaphoreType.DMA
    vmem = pl.BlockSpec(memory_space=pltpu.VMEM)
    anywhere = pl.BlockSpec(memory_space=pltpu.HBM)
    block = pltpu.VMEM((rows, width), f32)
    by_seq = pltpu.VMEM((steps, 4, rows), f32)
    by_group = pltpu.VMEM((devices, 4, rows), f32)
    by_device = pltpu.VMEM((steps, replicas, 4, rows), f32)
    spectrum = pltpu.VMEM((steps, pairs, 8, double), f32)
    taps_spectrum = pltpu.VMEM((steps, 8, double), f32)
    input_part, gate_part, filter_part = pl.pallas_call(
        functools.partial(kernel, steps, replicas, replicas * inputs.shape[0]),
        out_shape=(
            jax.ShapeDtypeStruct((rows, width), f32),
            jax.ShapeDtypeStruct((rows, width), f32),
            jax.ShapeDtypeStruct((width // replicas, rows), f32),
        ),
        in_specs=[anywhere] * 9,
        out_specs=(vmem, vmem, vmem),
        scratch_shapes=[block, block, block, block, pltpu.VMEM((1, width), f32)]
        + [pltpu.VMEM((rows, double), bf16)] * 2
        + [pltpu.VMEM((double, rows), bf16)] * 2
        + [pltpu.VMEM((replicas, width // replicas, rows), f32), by_seq, by_seq]
        + [by_group, by_device, by_group, by_device]
        + [pltpu.VMEM((steps * pairs, 8, rows), f32), pltpu.VMEM((steps, 8, rows), f32)]
        + [taps_spectrum, spectrum, spectrum, spectrum, taps_spectrum]
        + [by_device, by_group, by_device, by_group, by_seq, by_seq]
        + [pltpu.VMEM((width // 8, 8, rows), f32), dma((9,))]
        + [dma((n,)) for n in [steps] * 2 + [devices] * 8 + [steps] * 2],
        compiler_params=pltpu.CompilerParams(
            collective_id=0, has_side_effects=True, vmem_limit_bytes=60 * 1024 * 1024
        ),
    )(
        inputs[0], gate_values[0], out_grad[0], filter_taps, skip_gain[None, :],
        *[jnp.asarray(table) for table in tables],
    )
    return input_part[None], gate_part[None], filter_part.T


def solution(mesh):
    placed = (P("dp", "seq", None), P("dp", "seq", None), P("dp", "seq", None), P("seq", None), P())
    steps, replicas = mesh.shape["seq"], mesh.shape["dp"]

    def either(inputs, gate_values, out_grad, filter_taps, skip_gain):
        rows, width = filter_taps.shape
        fits = width == 4 * steps * replicas and replicas % 2 == 0 and rows % 128 == 0 and steps <= 8
        if fits and inputs.shape[0] == 1:
            return fused(inputs, gate_values, out_grad, filter_taps, skip_gain, steps, replicas)
        return local(inputs, gate_values, out_grad, filter_taps, skip_gain)

    return jax.shard_map(
        either,
        mesh=mesh,
        in_specs=placed,
        out_specs=(P("dp", "seq", None), P("dp", "seq", None), P("seq", "dp")),
        check_vma=False,
    )
```

profile of v0, /device:TPU:0, one launch (start us, length us, event | category | flops | bytes accessed | tf_op | source)
XLA Modules:
  0.0 43.7 jit_solution(3235170769029379070)
XLA Ops:
  0.6 39.8 %shard_map.112 = (f32[512,128]{1,0:T(8,128)}, f32[512,128]{1,0:T(8,128)}, f32[32,512]{1,0:T(8,128)}) custom-call(f32[512,128]{1,0:T(8,128)} %bitcast.9, f32[512,128]{1,0:T(8,128)} %bitcast.10, f32[512,128]{1,0:T(8,128)} %bitcast.11, f32[512,128]{1,0:T(8,128)} %taps_any.1, f32[1,128]{1,0:T(1,128)} %bitcast.13, bf16[512,1024]{1,0:T(8,128)(2,1)} %constant.8.clone.fh_any, ...), custom_call_target="tpu_custom_call" | custom-call | tf_op jit(solution)/shard_map/pallas_call | solution.py:476
  40.4 0.0 copy-start
  40.4 1.7 %copy.15 = f32[1,512,128]{2,1,0:T(8,128)} copy(f32[1,512,128]{2,1,0:T(8,128)} %bitcast.8) | data formatting | bytes 524288
  42.2 0.0 copy-done
  42.2 0.0 copy-start.1
  42.2 0.7 %copy.16 = f32[1,512,128]{2,1,0:T(8,128)} copy(f32[1,512,128]{2,1,0:T(8,128)S(1)} %bitcast.7) | data formatting | bytes 524288
  42.9 0.2 copy-done.1
  43.0 0.6 %copy.17 = f32[512,32]{0,1:T(8,128)} copy(f32[512,32]{0,1:T(8,128)S(1)} %bitcast.12) | data formatting | bytes 131072
Async XLA Ops:
  40.4 1.7 %copy-start = (f32[512,128]{1,0:T(8,128)S(1)}, f32[512,128]{1,0:T(8,128)}, u32[]{:S(2)}) copy-start(f32[512,128]{1,0:T(8,128)} %get-tuple-element.7) | copy-start | bytes 786436
  42.2 0.9 %copy-start.1 = (f32[32,512]{1,0:T(8,128)S(1)}, f32[32,512]{1,0:T(8,128)}, u32[]{:S(2)}) copy-start(f32[32,512]{1,0:T(8,128)} %get-tuple-element.8) | copy-start | bytes 196612
where the time goes:
time: 43.8 us; the launch traced here: 43.7 us
  Pallas kernels  39.8 us (91%)
  local copies, waits for them, and re-layouts  3.21 us (7%)
  between operations  0.65 us (1%)
    pallas_call x1, Pallas kernels, fused(): pl.pallas_call(functools.partial(kernel, steps, replicas, replicas * inpu...  39.8 us
    unnamed x7, local copies, waits for them, and re-layouts  3.21 us

commit v1 on v0

--- a/solution.py
+++ b/solution.py
@@ -211,13 +211,13 @@
 def kernel(
     steps, replicas, batch_total,
     in_any, gate_any, og_any, taps_any, skip_any, fh_any, fl_any, ih_any, il_any,
-    ig_ref, gg_ref, fg_ref,
+    ig_any, gg_any, fg_any,
     inp, gate, og, taps, skip, fh, fl, ih, il,
     tall, tsend, trecv, xsend, xrecv, gsend, grecv,
     rows8, trows8, spec_t, spec_x, spec_g, prod, tprod,
     csend, crecv, rsend, rrecv, bsend, brecv, merged,
     load_sem, tsend_sem, trecv_sem, xsend_sem, xrecv_sem, gsend_sem, grecv_sem,
-    csend_sem, crecv_sem, rsend_sem, rrecv_sem, bsend_sem, brecv_sem,
+    csend_sem, crecv_sem, rsend_sem, rrecv_sem, bsend_sem, brecv_sem, store_sem,
 ):
     devices = steps * replicas
     pairs = replicas // 2
@@ -439,12 +439,19 @@
 
     over_all(lambda p: back_copy(*c_refs, p, p).wait_recv())
     gain = skip[...]
-    gg_ref[...] = og[...] * (to_positions(crecv) + gain * inp[...])
+    og[...] = og[...] * (to_positions(crecv) + gain * inp[...])
+    stores = [
+        pltpu.make_async_copy(src, dst, store_sem.at[k])
+        for k, (src, dst) in enumerate([(og, gg_any), (gate, ig_any), (tall.at[0], fg_any)])
+    ]
+    stores[0].start()
     over_all(lambda p: back_copy(*r_refs, p, p).wait_recv())
-    ig_ref[...] = to_positions(rrecv) + gain * gate[...]
+    gate[...] = to_positions(rrecv) + gain * gate[...]
+    stores[1].start()
     over_seq(lambda s: seq_copy(*b_refs, s, s).wait_recv())
     scale = 1.0 / math.sqrt(batch_total * rows * steps)
-    fg_ref[...] = scale * jnp.concatenate([brecv[k] for k in range(steps)], axis=0)
+    tall[0] = scale * jnp.concatenate([brecv[k] for k in range(steps)], axis=0)
+    stores[2].start()
 
     over_seq(lambda s: seq_copy(*t_refs, s, s).wait_send())
     over_seq(lambda s: seq_copy(*b_refs, s, s).wait_send())
@@ -452,6 +459,16 @@
     over_all(lambda p: out_copy(*g_refs, p, p).wait_send())
     over_all(lambda p: back_copy(*c_refs, p, p).wait_send())
     over_all(lambda p: back_copy(*r_refs, p, p).wait_send())
+    for copy in stores:
+        copy.wait()
+
+
+def hand_over(*refs):
+    moves = [pltpu.make_async_copy(refs[k], refs[3 + k], refs[6].at[k]) for k in range(3)]
+    for copy in moves:
+        copy.start()
+    for copy in moves:
+        copy.wait()
 
 
 stride = 1
@@ -465,7 +482,6 @@
     tables = block_tables(rows)
     f32, bf16 = jnp.float32, jnp.bfloat16
     dma = pltpu.SemaphoreType.DMA
-    vmem = pl.BlockSpec(memory_space=pltpu.VMEM)
     anywhere = pl.BlockSpec(memory_space=pltpu.HBM)
     block = pltpu.VMEM((rows, width), f32)
     by_seq = pltpu.VMEM((steps, 4, rows), f32)
@@ -473,7 +489,7 @@
     by_device = pltpu.VMEM((steps, replicas, 4, rows), f32)
     spectrum = pltpu.VMEM((steps, pairs, 8, double), f32)
     taps_spectrum = pltpu.VMEM((steps, 8, double), f32)
-    input_part, gate_part, filter_part = pl.pallas_call(
+    results = pl.pallas_call(
         functools.partial(kernel, steps, replicas, replicas * inputs.shape[0]),
         out_shape=(
             jax.ShapeDtypeStruct((rows, width), f32),
@@ -481,7 +497,7 @@
             jax.ShapeDtypeStruct((width // replicas, rows), f32),
         ),
         in_specs=[anywhere] * 9,
-        out_specs=(vmem, vmem, vmem),
+        out_specs=(anywhere, anywhere, anywhere),
         scratch_shapes=[block, block, block, block, pltpu.VMEM((1, width), f32)]
         + [pltpu.VMEM((rows, double), bf16)] * 2
         + [pltpu.VMEM((double, rows), bf16)] * 2
@@ -491,7 +507,7 @@
         + [taps_spectrum, spectrum, spectrum, spectrum, taps_spectrum]
         + [by_device, by_group, by_device, by_group, by_seq, by_seq]
         + [pltpu.VMEM((width // 8, 8, rows), f32), dma((9,))]
-        + [dma((n,)) for n in [steps] * 2 + [devices] * 8 + [steps] * 2],
+        + [dma((n,)) for n in [steps] * 2 + [devices] * 8 + [steps] * 2 + [3]],
         compiler_params=pltpu.CompilerParams(
             collective_id=0, has_side_effects=True, vmem_limit_bytes=60 * 1024 * 1024
         ),
@@ -499,6 +515,14 @@
         inputs[0], gate_values[0], out_grad[0], filter_taps, skip_gain[None, :],
         *[jnp.asarray(table) for table in tables],
     )
+    input_part, gate_part, filter_part = pl.pallas_call(
+        hand_over,
+        out_shape=tuple(jax.ShapeDtypeStruct(part.shape, part.dtype) for part in results),
+        in_specs=[anywhere] * 3,
+        out_specs=(anywhere,) * 3,
+        scratch_shapes=[dma((3,))],
+        compiler_params=pltpu.CompilerParams(vmem_limit_bytes=60 * 1024 * 1024),
+    )(*results)
     return input_part[None], gate_part[None], filter_part.T
 
 

time: 43.8 us -> 58.8 us (1.34)
  Pallas kernels: 39.8 us -> 58 us
  local copies, waits for them, and re-layouts: 3.21 us -> 0 us
    pallas_call x0 -> x1, Pallas kernels: none -> 19 us  [fused(): pl.pallas_call(hand_over, out_shape=tuple((jax.ShapeDtypeStruct(part.shap...]
    unnamed x7 -> x0, local copies, waits for them, and re-layouts: 3.21 us -> none
    pallas_call x1, Pallas kernels: 39.8 us -> 39 us  [fused(): pl.pallas_call(functools.partial(kernel, steps, replicas, replicas * inpu...]
where the time goes in v1:
time: 58.8 us; the launch traced here: 58.6 us
  Pallas kernels  58 us (99%)
  between operations  0.64 us (1%)
    pallas_call x1, Pallas kernels, fused(): pl.pallas_call(functools.partial(kernel, steps, replicas, replicas * inpu...  39 us
    pallas_call x1, Pallas kernels, fused(): pl.pallas_call(hand_over, out_shape=tuple((jax.ShapeDtypeStruct(part.shap...  19 us

profile of v1, /device:TPU:0, one launch (start us, length us, event | category | flops | bytes accessed | tf_op | source)
XLA Modules:
  0.0 58.6 jit_solution(1466738995670336802)
XLA Ops:
  0.6 39.0 %shard_map.112 = (f32[512,128]{1,0:T(8,128)}, f32[512,128]{1,0:T(8,128)}, f32[32,512]{1,0:T(8,128)}) custom-call(f32[512,128]{1,0:T(8,128)} %bitcast.7, f32[512,128]{1,0:T(8,128)} %bitcast.8, f32[512,128]{1,0:T(8,128)} %bitcast.9, f32[512,128]{1,0:T(8,128)} %taps_any.1, f32[1,128]{1,0:T(1,128)} %bitcast.10, bf16[512,1024]{1,0:T(8,128)(2,1)} %constant.8.clone.fh_any, ...), custom_call_target="tpu_custom_call" | custom-call | tf_op jit(solution)/shard_map/pallas_call | solution.py:492
  39.6 19.0 %shard_map.113 = (f32[512,128]{1,0:T(8,128)}, f32[512,128]{1,0:T(8,128)}, f32[32,512]{1,0:T(8,128)}) custom-call(f32[512,128]{1,0:T(8,128)} %get-tuple-element.9.refs_0_, f32[512,128]{1,0:T(8,128)} %get-tuple-element.10.refs_1_, f32[32,512]{1,0:T(8,128)} %get-tuple-element.11.refs_2_), custom_call_target="tpu_custom_call" | custom-call | tf_op jit(solution)/shard_map/pallas_call | solution.py:518

commit v2 on v1

--- a/solution.py
+++ b/solution.py
@@ -464,10 +464,14 @@
 
 
 def hand_over(*refs):
-    moves = [pltpu.make_async_copy(refs[k], refs[3 + k], refs[6].at[k]) for k in range(3)]
-    for copy in moves:
+    reads = [pltpu.make_async_copy(refs[k], refs[6 + k], refs[9].at[k]) for k in range(3)]
+    writes = [pltpu.make_async_copy(refs[6 + k], refs[3 + k], refs[9].at[3 + k]) for k in range(3)]
+    for copy in reads:
         copy.start()
-    for copy in moves:
+    for read, write in zip(reads, writes):
+        read.wait()
+        write.start()
+    for copy in writes:
         copy.wait()
 
 
@@ -520,7 +524,7 @@
         out_shape=tuple(jax.ShapeDtypeStruct(part.shape, part.dtype) for part in results),
         in_specs=[anywhere] * 3,
         out_specs=(anywhere,) * 3,
-        scratch_shapes=[dma((3,))],
+        scratch_shapes=[pltpu.VMEM(part.shape, part.dtype) for part in results] + [dma((6,))],
         compiler_params=pltpu.CompilerParams(vmem_limit_bytes=60 * 1024 * 1024),
     )(*results)
     return input_part[None], gate_part[None], filter_part.T

time: 58.8 us -> 41.6 us (0.71)
  Pallas kernels: 58 us -> 40.8 us
    pallas_call x1, Pallas kernels: 19 us -> 1.8 us  [fused(): pl.pallas_call(hand_over, out_shape=tuple((jax.ShapeDtypeStruct(part.shap...]
where the time goes in v2:
time: 41.6 us; the launch traced here: 41.4 us
  Pallas kernels  40.8 us (98%)
  between operations  0.64 us (2%)
    pallas_call x1, Pallas kernels, fused(): pl.pallas_call(functools.partial(kernel, steps, replicas, replicas * inpu...  39 us
    pallas_call x1, Pallas kernels, fused(): pl.pallas_call(hand_over, out_shape=tuple((jax.ShapeDtypeStruct(part.shap...  1.8 us

profile of v2, /device:TPU:0, one launch (start us, length us, event | category | flops | bytes accessed | tf_op | source)
XLA Modules:
  0.0 41.4 jit_solution(17450962835142475276)
XLA Ops:
  0.6 39.0 %shard_map.112 = (f32[512,128]{1,0:T(8,128)}, f32[512,128]{1,0:T(8,128)}, f32[32,512]{1,0:T(8,128)}) custom-call(f32[512,128]{1,0:T(8,128)} %bitcast.7, f32[512,128]{1,0:T(8,128)} %bitcast.8, f32[512,128]{1,0:T(8,128)} %bitcast.9, f32[512,128]{1,0:T(8,128)} %taps_any.1, f32[1,128]{1,0:T(1,128)} %bitcast.10, bf16[512,1024]{1,0:T(8,128)(2,1)} %constant.8.clone.fh_any, ...), custom_call_target="tpu_custom_call" | custom-call | tf_op jit(solution)/shard_map/pallas_call | solution.py:496
  39.6 1.8 %shard_map.113 = (f32[512,128]{1,0:T(8,128)}, f32[512,128]{1,0:T(8,128)}, f32[32,512]{1,0:T(8,128)}) custom-call(f32[512,128]{1,0:T(8,128)} %get-tuple-element.9.refs_0_, f32[512,128]{1,0:T(8,128)} %get-tuple-element.10.refs_1_, f32[32,512]{1,0:T(8,128)} %get-tuple-element.11.refs_2_), custom_call_target="tpu_custom_call" | custom-call | tf_op jit(solution)/shard_map/pallas_call | solution.py:522

commit v3 on v2

--- a/solution.py
+++ b/solution.py
@@ -245,9 +245,9 @@
             (fh_any, fh), (fl_any, fl), (ih_any, ih), (il_any, il),
         ])
     ]
+    lax.fori_loop(1, devices, greet, 0)
     for copy in loads:
         copy.start()
-    lax.fori_loop(1, devices, greet, 0)
 
     def seq_copy(src, dst, src_sem, dst_sem, s, q):
         return pltpu.make_async_remote_copy(
@@ -436,6 +436,9 @@
     crecv[group] = csend[own_s, own_d]
     rrecv[group] = rsend[own_s, own_d]
     brecv[own_s] = bsend[own_s]
+    over_seq(lambda s: seq_copy(*t_refs, s, s).wait_send())
+    over_all(lambda p: out_copy(*x_refs, p, p).wait_send())
+    over_all(lambda p: out_copy(*g_refs, p, p).wait_send())
 
     over_all(lambda p: back_copy(*c_refs, p, p).wait_recv())
     gain = skip[...]
@@ -445,6 +448,7 @@
         for k, (src, dst) in enumerate([(og, gg_any), (gate, ig_any), (tall.at[0], fg_any)])
     ]
     stores[0].start()
+    over_all(lambda p: back_copy(*c_refs, p, p).wait_send())
     over_all(lambda p: back_copy(*r_refs, p, p).wait_recv())
     gate[...] = to_positions(rrecv) + gain * gate[...]
     stores[1].start()
@@ -453,11 +457,7 @@
     tall[0] = scale * jnp.concatenate([brecv[k] for k in range(steps)], axis=0)
     stores[2].start()
 
-    over_seq(lambda s: seq_copy(*t_refs, s, s).wait_send())
     over_seq(lambda s: seq_copy(*b_refs, s, s).wait_send())
-    over_all(lambda p: out_copy(*x_refs, p, p).wait_send())
-    over_all(lambda p: out_copy(*g_refs, p, p).wait_send())
-    over_all(lambda p: back_copy(*c_refs, p, p).wait_send())
     over_all(lambda p: back_copy(*r_refs, p, p).wait_send())
     for copy in stores:
         copy.wait()

time: 41.6 us -> 40.9 us (0.983)
  Pallas kernels: 40.8 us -> 40.1 us
    pallas_call x1, Pallas kernels: 39 us -> 38.3 us  [fused(): pl.pallas_call(functools.partial(kernel, steps, replicas, replicas * inpu...]
where the time goes in v3:
time: 40.9 us; the launch traced here: 40.7 us
  Pallas kernels  40.1 us (98%)
  between operations  0.64 us (2%)
    pallas_call x1, Pallas kernels, fused(): pl.pallas_call(functools.partial(kernel, steps, replicas, replicas * inpu...  38.3 us
    pallas_call x1, Pallas kernels, fused(): pl.pallas_call(hand_over, out_shape=tuple((jax.ShapeDtypeStruct(part.shap...  1.8 us

profile of v3, /device:TPU:0, one launch (start us, length us, event | category | flops | bytes accessed | tf_op | source)
XLA Modules:
  0.0 40.7 jit_solution(16491729371720553179)
XLA Ops:
  0.6 38.3 %shard_map.112 = (f32[512,128]{1,0:T(8,128)}, f32[512,128]{1,0:T(8,128)}, f32[32,512]{1,0:T(8,128)}) custom-call(f32[512,128]{1,0:T(8,128)} %bitcast.7, f32[512,128]{1,0:T(8,128)} %bitcast.8, f32[512,128]{1,0:T(8,128)} %bitcast.9, f32[512,128]{1,0:T(8,128)} %taps_any.1, f32[1,128]{1,0:T(1,128)} %bitcast.10, bf16[512,1024]{1,0:T(8,128)(2,1)} %constant.8.clone.fh_any, ...), custom_call_target="tpu_custom_call" | custom-call | tf_op jit(solution)/shard_map/pallas_call | solution.py:496
  38.9 1.8 %shard_map.113 = (f32[512,128]{1,0:T(8,128)}, f32[512,128]{1,0:T(8,128)}, f32[32,512]{1,0:T(8,128)}) custom-call(f32[512,128]{1,0:T(8,128)} %get-tuple-element.9.refs_0_, f32[512,128]{1,0:T(8,128)} %get-tuple-element.10.refs_1_, f32[32,512]{1,0:T(8,128)} %get-tuple-element.11.refs_2_), custom_call_target="tpu_custom_call" | custom-call | tf_op jit(solution)/shard_map/pallas_call | solution.py:522
